TPU v7x, 512 devices: a whole 4x8x8 slice. The times are simulated.
512 devices in a mesh: ctx: 64 (over y, z_hi, core), tp: 8 (over z_lo, x).
Axes of the slice: x: 4, y: 8, z: 8 (z_hi: 4, z_lo: 2; z = z_hi * 2 + z_lo), core: 2. Of those that a mesh axis runs over, the one named last changes fastest.
Arguments:
- queries: bfloat16 [8192, 4096], P('ctx', 'tp'), may hold values from -13.5 to 13.5
- keys: bfloat16 [8192, 1024], P('ctx', 'tp'), may hold values from -4 to 4
- values: bfloat16 [8192, 1024], P('ctx', 'tp'), may hold values from -6 to 6
- saved_out: bfloat16 [8192, 4096], P('ctx', 'tp'), may hold values from -4 to 4
- grad_out: bfloat16 [8192, 4096], P('ctx', 'tp'), may hold values from -48 to 48
- layer_in: bfloat16 [8192, 4096], P('ctx'), may hold values from -6 to 6
Outputs:
- grad_queries: bfloat16 [8192, 4096], P('ctx', 'tp')
- key_gradient: bfloat16 [8192, 1024], P('ctx', 'tp')
- value_gradient: bfloat16 [8192, 1024], P('ctx', 'tp')
- value_weight_direction: bfloat16 [4096, 1024], P('ctx', 'tp')
All inputs are finite; a program needn't handle non-finite values.
Results may differ from a plain program's by a relative error of at most 0.0055.
The roundings to bfloat16 on the way count: a program that leaves them out, or rounds other values in their place, can miss the bound.
Values may be sent and summed in bfloat16 or wider, within the bound.
A program may use at most 64 MiB of HBM per device.

v0:
```python
import jax
import jax.numpy as jnp
from jax import lax
from jax.sharding import PartitionSpec as P

HEAD_SIZE = 128
SHAMPOO_ROWS = 512
NEWTON = 2


masked_fill = -1e30
highest = lax.Precision.HIGHEST


def score_block(query_tensor4, rows_of_keys, query_first, key_first, score_scale):
    scores = (
        jnp.einsum(
            "lcfa,vca->cflv", query_tensor4, rows_of_keys, preferred_element_type=jnp.float32
        )
        * score_scale
    )
    tile_shape = (query_tensor4.shape[0], rows_of_keys.shape[0])
    query_pos = query_first + lax.broadcasted_iota(jnp.int32, tile_shape, 0)
    key_pos = key_first + lax.broadcasted_iota(jnp.int32, tile_shape, 1)
    return (scores, (key_pos <= query_pos)[None, None])


def merge_stats(row_stats, query_tensor4, rows_of_keys, query_first, key_first, score_scale):
    row_max, row_total = row_stats
    scores, visible = score_block(query_tensor4, rows_of_keys, query_first, key_first, score_scale)
    masked = jnp.where(visible, scores, masked_fill)
    new_max = jnp.maximum(row_max, jnp.max(masked, axis=-1))
    weights = jnp.where(visible, jnp.exp(masked - new_max[..., None]), 0.0)
    row_total = row_total * jnp.exp(row_max - new_max) + jnp.sum(weights, axis=-1)
    return (new_max, row_total)


def matmul_high(first_mat, second_mat):
    return jnp.matmul(first_mat, second_mat, precision=highest)


def inverse_root(statistic):
    dim_size = statistic.shape[-1]
    identity = jnp.eye(dim_size, dtype=jnp.float32)
    matrix = statistic / jnp.sqrt(jnp.sum(statistic * statistic, axis=(1, 2), keepdims=True))
    root_est = jnp.broadcast_to(identity, statistic.shape)
    for iteration in range(NEWTON):
        factor = (5.0 * identity - matrix) * 0.25
        root_est = matmul_high(root_est, factor)
        square = matmul_high(factor, factor)
        matrix = matmul_high(matmul_high(square, square), matrix)
    return root_est


def fold_sources(received, ctx_size, tok_rows):
    return jnp.sum(received.reshape(ctx_size, tok_rows, received.shape[1]), axis=0).astype(
        jnp.bfloat16
    )


def weight_block(layer_in, value_gradient):
    local_term = lax.dot_general(
        layer_in, value_gradient, (((0,), (0,)), ((), ())), preferred_element_type=jnp.float32
    )
    ctx_size = lax.axis_size("ctx")
    own_rows = layer_in.shape[1] // ctx_size
    position = lax.axis_index("ctx")
    row_first = position * own_rows
    block_first = row_first // SHAMPOO_ROWS * SHAMPOO_ROWS
    weight_gradient = lax.psum(local_term, "ctx")
    return lax.dynamic_slice_in_dim(weight_gradient, block_first, SHAMPOO_ROWS, 0)


def per_device(queries, keys, values, saved_out, grad_out, layer_in):
    tok_rows = queries.shape[0]
    kv_width = keys.shape[1]
    kv_heads = kv_width // HEAD_SIZE
    q_heads = queries.shape[1] // HEAD_SIZE
    heads_per_group = q_heads // kv_heads
    ctx_size = lax.axis_size("ctx")
    sequence_length = tok_rows * ctx_size
    key_block = min(512, sequence_length)
    score_scale = HEAD_SIZE ** (-0.5)
    query_first = lax.axis_index("ctx") * tok_rows
    block_count = (query_first + tok_rows - 1) // key_block + 1
    query_tensor4 = queries.reshape(tok_rows, kv_heads, heads_per_group, HEAD_SIZE)
    output_gradient4 = grad_out.reshape(tok_rows, kv_heads, heads_per_group, HEAD_SIZE)
    stat_shape = (kv_heads, heads_per_group, tok_rows)
    start_stats = (
        jnp.full(stat_shape, masked_fill, jnp.float32),
        jnp.zeros(stat_shape, jnp.float32),
    )
    key_all, value_all = (
        lax.all_gather(keys, "ctx", axis=0, tiled=True),
        lax.all_gather(values, "ctx", axis=0, tiled=True),
    )

    def forward_turn(number, row_stats):
        key_first = number * key_block
        rows_of_keys = lax.dynamic_slice_in_dim(key_all, key_first, key_block, 0).reshape(
            key_block, kv_heads, HEAD_SIZE
        )
        return merge_stats(
            row_stats, query_tensor4, rows_of_keys, query_first, key_first, score_scale
        )

    row_max, row_total = lax.fori_loop(0, block_count, forward_turn, start_stats)
    log_total = row_max + jnp.log(row_total)
    row_delta = jnp.sum(
        output_gradient4.astype(jnp.float32)
        * saved_out.reshape(tok_rows, kv_heads, heads_per_group, HEAD_SIZE).astype(jnp.float32),
        axis=-1,
    ).transpose(1, 2, 0)
    zero_parts = jnp.zeros((sequence_length, kv_width), jnp.float32)

    def backward_turn(number, folded):
        grad_acc, key_parts, value_parts = folded
        key_first = number * key_block
        rows_of_keys = lax.dynamic_slice_in_dim(key_all, key_first, key_block, 0).reshape(
            key_block, kv_heads, HEAD_SIZE
        )
        rows_of_values = lax.dynamic_slice_in_dim(value_all, key_first, key_block, 0).reshape(
            key_block, kv_heads, HEAD_SIZE
        )
        scores, visible = score_block(
            query_tensor4, rows_of_keys, query_first, key_first, score_scale
        )
        prob_full = jnp.where(visible, jnp.exp(scores - log_total[..., None]), 0.0)
        probs_reduced = prob_full.astype(jnp.bfloat16)
        dprobs = jnp.einsum(
            "lcfa,vca->cflv", output_gradient4, rows_of_values, preferred_element_type=jnp.float32
        )
        score_gradient = (prob_full * (dprobs - row_delta[..., None]) * score_scale).astype(
            jnp.bfloat16
        )
        grad_acc = grad_acc + jnp.einsum(
            "mfyi,imz->ymfz", score_gradient, rows_of_keys, preferred_element_type=jnp.float32
        )
        key_term = jnp.einsum(
            "cmvn,vcmx->ncx", score_gradient, query_tensor4, preferred_element_type=jnp.float32
        ).reshape(key_block, kv_width)
        value_term = jnp.einsum(
            "cmvn,vcmx->ncx", probs_reduced, output_gradient4, preferred_element_type=jnp.float32
        ).reshape(key_block, kv_width)
        key_parts = lax.dynamic_update_slice_in_dim(key_parts, key_term, key_first, 0)
        value_parts = lax.dynamic_update_slice_in_dim(value_parts, value_term, key_first, 0)
        return (grad_acc, key_parts, value_parts)

    grad_start = jnp.zeros((tok_rows, kv_heads, heads_per_group, HEAD_SIZE), jnp.float32)
    grad_acc, key_parts, value_parts = lax.fori_loop(
        0, block_count, backward_turn, (grad_start, zero_parts, zero_parts)
    )
    grad_queries = grad_acc.reshape(tok_rows, q_heads * HEAD_SIZE).astype(jnp.bfloat16)
    got_keys, got_values = (
        lax.all_to_all(key_parts, "ctx", split_axis=0, concat_axis=0, tiled=True),
        lax.all_to_all(value_parts, "ctx", split_axis=0, concat_axis=0, tiled=True),
    )
    key_gradient = fold_sources(got_keys, ctx_size, tok_rows)
    value_gradient = fold_sources(got_values, ctx_size, tok_rows)
    summed_block = weight_block(layer_in, value_gradient)
    model_width = layer_in.shape[1]
    own_rows = model_width // ctx_size
    row_first = lax.axis_index("ctx") * own_rows
    block_first = row_first // SHAMPOO_ROWS * SHAMPOO_ROWS
    grad_block = summed_block.reshape(SHAMPOO_ROWS, kv_heads, HEAD_SIZE).transpose(1, 0, 2)
    squares = jnp.sum(grad_block * grad_block, axis=(1, 2), keepdims=True)
    transposed = jnp.swapaxes(grad_block, 1, 2)
    left_stat = matmul_high(grad_block, transposed) + (
        0.1 * squares / SHAMPOO_ROWS + 1e-06
    ) * jnp.eye(SHAMPOO_ROWS, dtype=jnp.float32)
    right_stat = matmul_high(transposed, grad_block) + (
        0.1 * squares / HEAD_SIZE + 1e-06
    ) * jnp.eye(HEAD_SIZE, dtype=jnp.float32)
    precond = matmul_high(
        matmul_high(inverse_root(left_stat), grad_block), inverse_root(right_stat)
    )
    direction = precond / jnp.sqrt(jnp.mean(precond * precond, axis=(1, 2), keepdims=True) + 1e-06)
    own_part = lax.dynamic_slice_in_dim(direction, row_first - block_first, own_rows, 1)
    value_weight_direction = (
        own_part.transpose(1, 0, 2).reshape(own_rows, kv_width).astype(jnp.bfloat16)
    )
    return (grad_queries, key_gradient, value_gradient, value_weight_direction)


def solution(mesh):
    placed = (
        P("ctx", "tp"),
        P("ctx", "tp"),
        P("ctx", "tp"),
        P("ctx", "tp"),
        P("ctx", "tp"),
        P("ctx", None),
    )
    return jax.shard_map(
        per_device,
        mesh=mesh,
        in_specs=placed,
        out_specs=(P("ctx", "tp"), P("ctx", "tp"), P("ctx", "tp"), P("ctx", "tp")),
        check_vma=False,
    )
```

profile of v0, /device:TPU:1, one launch (start us, length us, event | category | flops | bytes accessed | tf_op | source)
XLA Modules:
  0.0 1069.4 jit_solution(3598652055827367294)
XLA Ops:
  8.7 1.0 copy.15
  9.8 1.0 copy.17
  10.9 1.0 copy.18
  12.1 90.1 %all-gather.3.cloned.1.call-done = bf16[8192,128]{1,0:T(8,128)(2,1)} async-done(((bf16[128,128]{1,0:T(8,128)(2,1)}), bf16[8192,128]{1,0:T(8,128)(2,1)}) %all-gather.3.cloned.1.call-update) | async-done | bytes 2097168 | tf_op jit(solution)/shard_map/all_gather | solution.py:94
  102.2 1.6 while.26
  102.3 1.2 fusion.118
  103.8 83.3 %all-gather.5.cloned.1.call-done = bf16[8192,128]{1,0:T(8,128)(2,1)} async-done(((bf16[128,128]{1,0:T(8,128)(2,1)}), bf16[8192,128]{1,0:T(8,128)(2,1)}) %all-gather.5.cloned.1.call-update) | async-done | bytes 2097168 | tf_op jit(solution)/shard_map/all_gather | solution.py:95
  187.2 2.2 broadcast_in_dim.59
  189.4 2.2 broadcast_in_dim.59.clone
  191.6 5.8 while.27
  191.8 1.3 fusion.129
  193.1 1.2 fusion.130
  194.3 1.0 fusion.132
  195.3 1.0 fusion.133
  196.3 1.2 fusion.131
  197.5 191.8 %all_to_all.18 = f32[64,128,128]{2,1,0:T(8,128)} all-to-all(f32[64,128,128]{2,1,0:T(8,128)} %bitcast.174), channel_id=1, replica_groups=mesh['ctx'=64,'tp'=8] {'ctx'}, dimensions={0} | all-to-all | bytes 8388608 | tf_op jit(solution)/shard_map/all_to_all | solution.py:156
  389.2 17.3 %all-to-all-start = ((f32[64,128,128]{2,1,0:T(8,128)}), f32[64,128,128]{2,1,0:T(8,128)}, u32[]{:S(2)}, u32[]{:S(2)}) async-start(f32[64,128,128]{2,1,0:T(8,128)} %bitcast.173), calls=%async_computation | async-start | bytes 8388608 | tf_op jit(solution)/shard_map/all_to_all | solution.py:155
  406.7 2.4 reduce_sum.79
  409.1 1.8 convolution_bitcast_fusion.4
  411.8 102.5 %all-to-all-done = f32[64,128,128]{2,1,0:T(8,128)} async-done(((f32[64,128,128]{2,1,0:T(8,128)}), f32[64,128,128]{2,1,0:T(8,128)}, u32[]{:S(2)}, u32[]{:S(2)}) %all-to-all-start) | async-done | bytes 4194336 | tf_op jit(solution)/shard_map/all_to_all | solution.py:155
  514.2 3.0 reduce_sum.78
  517.3 522.2 %all-reduce.2.cloned.1.call-done = f32[4096,128]{0,1:T(8,128)} async-done(((f32[4096,128]{0,1:T(8,128)}), f32[4096,128]{0,1:T(8,128)}) %all-reduce.2.cloned.1.call-update) | async-done | bytes 2097168 | tf_op jit(solution)/shard_map/psum | solution.py:70
  1039.5 1.6 multiply_reduce_fusion.2
  1041.8 2.1 multiply_reduce_fusion.3
  1045.7 2.8 multiply_reduce_fusion
  1049.2 2.0 fusion.37
  1051.2 1.2 fusion.36
  1052.8 1.8 fusion.81
  1054.7 1.9 fusion.33
  1056.8 1.8 fusion.82
  1058.6 1.9 fusion.49
  1060.6 1.0 multiply_reduce_fusion.1
  (35 shorter events, 5.0 us)
Async XLA Ops:
  7.2 402.0 %copy-start = (bf16[128,4096]{1,0:T(8,128)(2,1)S(1)}, bf16[128,4096]{1,0:T(8,128)(2,1)}, u32[]{:S(2)}) copy-start(bf16[128,4096]{1,0:T(8,128)(2,1)} %param.15) | copy-start | bytes 3145732
  7.2 95.0 %all-gather.3.cloned.1.call-start = ((), (), s32[]{:S(2)}) async-start(), calls=%async_computation.2 | async-start | bytes 2129920 | tf_op jit(solution)/shard_map/all_gather | solution.py:94
  7.9 179.2 %all-gather.5.cloned.1.call-start = ((), (), s32[]{:S(2)}) async-start(), calls=%async_computation.3 | async-start | bytes 2129920 | tf_op jit(solution)/shard_map/all_gather | solution.py:95
  389.2 125.0 %all-to-all-start = ((f32[64,128,128]{2,1,0:T(8,128)}), f32[64,128,128]{2,1,0:T(8,128)}, u32[]{:S(2)}, u32[]{:S(2)}) async-start(f32[64,128,128]{2,1,0:T(8,128)} %bitcast.173), calls=%async_computation | async-start | bytes 8388608 | tf_op jit(solution)/shard_map/all_to_all | solution.py:155
  406.5 633.0 %all-reduce.2.cloned.1.call-start = ((), (), s32[]{:S(2)}) async-start(), calls=%async_computation.4 | async-start | bytes 4194304 | tf_op jit(solution)/shard_map/psum | solution.py:70
  409.1 1.8 copy-start.1
Sparse Core Ops, SparseCore 0:
  11.3 90.7 all-gather.2
  105.5 81.6 all-gather.4
  411.0 628.4 all-reduce.1
where the time goes:
time: 1070 us
  waiting for transfers between devices  800 us (75%)
  blocking collectives  192 us (18%)
  matrix products  26.2 us (2%)
  starting transfers between devices  17.6 us (2%)
  between operations  17.4 us (2%)
    psum x1, waiting for transfers between devices, weight_block(): weight_gradient = lax.psum(local_term, 'ctx')  522 us
    all_to_all x1, blocking collectives, per_device(): lax.all_to_all(value_parts, 'ctx', split_axis=0, concat_axis=0, tiled=True)  192 us
    all_to_all x1, waiting for transfers between devices, per_device(): lax.all_to_all(key_parts, 'ctx', split_axis=0, concat_axis=0, tiled=True)  102 us
    all_gather x1, waiting for transfers between devices, per_device(): lax.all_gather(keys, 'ctx', axis=0, tiled=True)  90.1 us
    all_gather x1, waiting for transfers between devices, per_device(): lax.all_gather(values, 'ctx', axis=0, tiled=True)  83.3 us
  transfers between devices with their start and end apart: 4, of which 4 were waited for; matrix products, arithmetic and copies ran while one was open for 1% of the time, Pallas kernels for 0%

commit v1 on v0

v1 whole, which is shorter than its diff:
```python
import functools

import jax
import jax.numpy as jnp
from jax import lax
from jax.experimental import pallas as pl
from jax.experimental.pallas import tpu as pltpu
from jax.sharding import PartitionSpec as P

HEAD = 128
Y, Z, CORES = 8, 4, 2
HEADS = 4
ROWS = 256
ALL_ROWS = HEADS * ROWS
CHUNK = Z * 128
NEWTON = 2
BLOCK_ROWS = 512
FILL = -1e30
SCALE = HEAD ** (-0.5)
SCALE2 = SCALE * 1.4426950408889634
HIGHEST = lax.Precision.HIGHEST
F32 = jnp.float32
BF16 = jnp.bfloat16

KZ, VZ, SIB, RK, RV, LSE, SV, SK, ZV, ZK, DQ, WC, WY, WZ, GC, N_SEMS = (
    0, 3, 6, 18, 25, 32, 33, 40, 47, 50, 53, 54, 55, 62, 65, 66,
)


def dot(a, b, dims=(((1,), (0,)), ((), ())), precision=None):
    return lax.dot_general(a, b, dims, precision=precision, preferred_element_type=F32)


def dot_high(a, b):
    return dot(a, b, precision=HIGHEST)


def kernel(
    q_ref, k_ref, v_ref, o_ref, do_ref, x_ref,
    dq_out, dk_out, dv_out, w_out,
    kbuf, vbuf, qs, dos, os, q_t, do_t, delta, m_run, l_run, lse, lse_in, dq_t,
    tmp_v, tmp_k, out_v, out_k, in_v, in_k, zout_v, zout_k, zin_v, zin_k,
    dq_keep, dq_send, dq_in, w_keep, w_send, w_in, wy_out, wy_in, wz_out, wz_in, g_out, g_in, p_scr,
    send, recv,
):
    c = lax.axis_index("ctx")
    core = lax.rem(c, 2)
    z = lax.rem(c // 2, Z)
    y = c // (2 * Z)

    def dev(yy, zz, cc):
        return {"ctx": (yy * Z + zz) * 2 + cc}

    sibling = dev(y, z, 1 - core)

    def at_y(step):
        return lax.rem(y + step + Y, Y)

    def at_z(step):
        return lax.rem(z + step, Z)

    def copy(src, dst, number, device):
        return pltpu.make_async_remote_copy(
            src_ref=src, dst_ref=dst, send_sem=send.at[number], recv_sem=recv.at[number],
            device_id=device, device_id_type=pl.DeviceIdType.MESH,
        )

    barrier = pltpu.get_barrier_semaphore()
    partners = [dev(at_y(i), z, core) for i in range(1, Y)]
    partners += [dev(y, at_z(i), core) for i in range(1, Z)] + [sibling]
    for partner in partners:
        pl.semaphore_signal(barrier, inc=1, device_id=partner, device_id_type=pl.DeviceIdType.MESH)
    pl.semaphore_wait(barrier, len(partners))

    kz = [copy(k_ref, kbuf.at[y, z], KZ + i - 1, dev(y, at_z(i), core)) for i in range(1, Z)]
    vz = [copy(v_ref, vbuf.at[y, z], VZ + i - 1, dev(y, at_z(i), core)) for i in range(1, Z)]
    for one in kz + vz:
        one.start()
    own_rows = [pl.ds(pl.multiple_of(h * ROWS + core * 128, 128), 128) for h in range(HEADS)]
    sib = []
    for n, (ref, buf) in enumerate(((q_ref, qs), (do_ref, dos), (o_ref, os))):
        for h in range(HEADS):
            sib.append(
                copy(ref.at[:, pl.ds(h * HEAD, HEAD)], buf.at[own_rows[h]], SIB + n * HEADS + h, sibling)
            )
    for one in sib:
        one.start()
    for ref, buf in ((q_ref, qs), (do_ref, dos), (o_ref, os)):
        for h in range(HEADS):
            buf[own_rows[h], :] = ref[:, h * HEAD : (h + 1) * HEAD]
    kbuf[y, z] = k_ref[...]
    vbuf[y, z] = v_ref[...]
    m_run[...] = jnp.full(m_run.shape, FILL, F32)
    l_run[...] = jnp.zeros(l_run.shape, F32)
    dq_t[...] = jnp.zeros(dq_t.shape, F32)
    for one in sib:
        one.wait_recv()
    for h in range(HEADS):
        rows = slice(h * ROWS, (h + 1) * ROWS)
        cot = dos[rows, :].astype(F32)
        q_t[:, rows] = qs[rows, :].astype(F32).T.astype(BF16)
        do_t[:, rows] = cot.T.astype(BF16)
        delta[:, rows] = jnp.broadcast_to(
            jnp.sum((cot * os[rows, :].astype(F32)).T, axis=0, keepdims=True), (8, ROWS)
        )

    def scores(keys, h, diagonal):
        s = dot(keys, q_t[:, h * ROWS : (h + 1) * ROWS]) * SCALE2
        if diagonal:
            key = lax.broadcasted_iota(jnp.int32, (CHUNK, ROWS), 0)
            key = key + (key >> 7) * 128 + core * 128
            row = lax.broadcasted_iota(jnp.int32, (CHUNK, ROWS), 1) + z * ROWS
            s = jnp.where(key <= row, s, FILL)
        return s

    def forward(chunk, diagonal):
        keys = kbuf[chunk].reshape(CHUNK, HEAD)
        for h in range(HEADS):
            cols = slice(h * ROWS, (h + 1) * ROWS)
            s = scores(keys, h, diagonal).reshape(CHUNK // 8, 8, ROWS)
            old = m_run[:, cols]
            new = jnp.maximum(old, jnp.max(s, axis=0))
            l_run[:, cols] = l_run[:, cols] * jnp.exp2(old - new) + jnp.sum(jnp.exp2(s - new[None]), axis=0)
            m_run[:, cols] = new

    def ring_copies(t):
        up = lax.rem(t, 2) == 0
        s = t // 2
        chunk = jnp.where(up, at_y(-s), at_y(s))
        target = dev(jnp.where(up, at_y(1), at_y(-1)), z, core)
        return [copy(buf.at[chunk], buf.at[chunk], base + t, target) for buf, base in ((kbuf, RK), (vbuf, RV))]

    def ring_waits(t):
        up = lax.rem(t, 2) == 0
        s = t // 2
        chunk = jnp.where(up, at_y(-1 - s), at_y(1 + s))
        waits = [copy(buf.at[chunk], buf.at[chunk], base + t, sibling) for buf, base in ((kbuf, RK), (vbuf, RV))]
        return chunk, waits

    for one in kz + vz:
        one.wait_recv()

    def gather_step(t, _):
        @pl.when(t >= 2)
        def _():
            _, waits = ring_waits(t - 2)
            for one in waits:
                one.wait_recv()

        for one in ring_copies(t):
            one.start()

        @pl.when(t == 0)
        def _():
            forward(y, True)

        @pl.when(t >= 2)
        def _():
            chunk, _ = ring_waits(t - 2)

            @pl.when(chunk < y)
            def _():
                forward(chunk, False)

        return 0

    lax.fori_loop(0, 7, gather_step, 0)

    def gather_end(t, _):
        chunk, waits = ring_waits(t)
        for one in waits:
            one.wait_recv()

        @pl.when(chunk < y)
        def _():
            forward(chunk, False)

        return 0

    lax.fori_loop(5, 7, gather_end, 0)

    top = jnp.max(m_run[...], axis=0, keepdims=True)
    total = jnp.sum(l_run[...] * jnp.exp2(m_run[...] - top), axis=0, keepdims=True)
    lse[...] = jnp.broadcast_to(top + jnp.log2(total), lse.shape)
    lse_copy = copy(lse, lse_in, LSE, sibling)
    lse_copy.start()
    lse_copy.wait()
    high = jnp.maximum(lse[...], lse_in[...])
    low = jnp.minimum(lse[...], lse_in[...])
    lse[...] = high + jnp.log2(1.0 + jnp.exp2(low - high))

    def backward(chunk, diagonal):
        keys = kbuf[chunk].reshape(CHUNK, HEAD)
        vals = vbuf[chunk].reshape(CHUNK, HEAD)
        keys_t = keys.astype(F32).T.astype(BF16)
        for h in range(HEADS):
            cols = slice(h * ROWS, (h + 1) * ROWS)
            p = jnp.exp2(scores(keys, h, diagonal) - lse[0:1, cols])
            dp = dot(vals, do_t[:, cols])
            ds = (p * (dp - delta[0:1, cols]) * SCALE).astype(BF16)
            dv = dot(p.astype(BF16), dos[cols, :])
            dk = dot(ds, qs[cols, :])
            if h == 0:
                tmp_v[...] = dv
                tmp_k[...] = dk
            else:
                tmp_v[...] += dv
                tmp_k[...] += dk
            dq_t[:, cols] += dot(keys_t, ds)

    def sum_copies(t):
        target = dev(jnp.where(lax.rem(t, 2) == 0, at_y(1), at_y(-1)), z, core)
        return [
            copy(out.at[t], into.at[t], base + t, target)
            for out, into, base in ((out_v, in_v, SV), (out_k, in_k, SK))
        ]

    def reduce_step(t, _):
        s = t // 2
        chunk = jnp.where(lax.rem(t, 2) == 0, at_y(4 - s), at_y(s - 3))

        @pl.when(chunk < y)
        def _():
            backward(chunk, False)

        @pl.when(chunk > y)
        def _():
            tmp_v[...] = jnp.zeros(tmp_v.shape, F32)
            tmp_k[...] = jnp.zeros(tmp_k.shape, F32)

        @pl.when(t >= 2)
        def _():
            for one in sum_copies(t - 2):
                one.wait_recv()
            tmp_v[...] += in_v[t - 2].astype(F32)
            tmp_k[...] += in_k[t - 2].astype(F32)

        out_v[t] = tmp_v[...].astype(BF16)
        out_k[t] = tmp_k[...].astype(BF16)
        for one in sum_copies(t):
            one.start()
        return 0

    lax.fori_loop(0, 7, reduce_step, 0)
    backward(y, True)

    for h in range(HEADS):
        full = dq_t[:, h * ROWS : (h + 1) * ROWS].T.reshape(2, 128, HEAD)
        tmp_rows = pl.ds(h * ROWS, ROWS)
        p_rows = full.reshape(ROWS, HEAD)
        p_scr[pl.ds(0, ROWS), :] = p_rows
        dq_keep[h] = p_scr[pl.ds(pl.multiple_of(core * 128, 128), 128), :]
        dq_send[h] = p_scr[pl.ds(pl.multiple_of((1 - core) * 128, 128), 128), :]
    dq_copy = copy(dq_send, dq_in, DQ, sibling)
    dq_copy.start()

    for t in (5, 6):
        for one in sum_copies(t):
            one.wait_recv()
    tmp_v[...] += in_v[5].astype(F32) + in_v[6].astype(F32)
    tmp_k[...] += in_k[5].astype(F32) + in_k[6].astype(F32)

    zc = []
    for tmp, out, into, base in ((tmp_v, zout_v, zin_v, ZV), (tmp_k, zout_k, zin_k, ZK)):
        for i in range(1, Z):
            rows = pl.ds(pl.multiple_of(at_z(i) * 128, 128), 128)
            out[i - 1] = tmp[rows, :].astype(BF16)
            one = copy(out.at[i - 1], into.at[i - 1], base + i - 1, dev(y, at_z(i), core))
            one.start()
            zc.append(one)
    mine = pl.ds(pl.multiple_of(z * 128, 128), 128)
    for one in zc[:3]:
        one.wait_recv()
    value_grad = tmp_v[mine, :]
    for i in range(Z - 1):
        value_grad = value_grad + zin_v[i].astype(F32)
    value_low = value_grad.astype(BF16)
    dv_out[...] = value_low
    value_t = value_low.astype(F32).T.astype(BF16)

    def weight_step(i, _):
        for ref, half in ((w_keep, core), (w_send, 1 - core)):
            cols = pl.ds(pl.multiple_of(i * BLOCK_ROWS + half * 256, 256), 256)
            ref[i] = dot(value_t, x_ref[:, cols])
        return 0

    lax.fori_loop(0, Y, weight_step, 0)
    wc = copy(w_send, w_in, WC, sibling)
    wc.start()

    for one in zc[3:]:
        one.wait_recv()
    key_grad = tmp_k[mine, :]
    for i in range(Z - 1):
        key_grad = key_grad + zin_k[i].astype(F32)
    dk_out[...] = key_grad.astype(BF16)
    dq_copy.wait_recv()
    for h in range(HEADS):
        dq_out[:, h * HEAD : (h + 1) * HEAD] = (dq_keep[h] + dq_in[h]).astype(BF16)

    wc.wait_recv()
    wy = []
    for i in range(1, Y):
        target = at_y(i)
        wy_out[i - 1] = (w_keep[target] + w_in[target]).astype(BF16)
        one = copy(wy_out.at[i - 1], wy_in.at[i - 1], WY + i - 1, dev(target, z, core))
        one.start()
        wy.append(one)
    g = w_keep[y] + w_in[y]
    for i in range(1, Y):
        wy[i - 1].wait_recv()
        g = g + wy_in[i - 1].astype(F32)
    wz_out[...] = g.astype(BF16)
    wz = [copy(wz_out, wz_in.at[i - 1], WZ + i - 1, dev(y, at_z(i), core)) for i in range(1, Z)]
    for one in wz:
        one.start()
    for i in range(1, Z):
        wz[i - 1].wait_recv()
        g = g + wz_in[i - 1].astype(F32)
    g_out[...] = g
    gc = copy(g_out, g_in, GC, sibling)
    gc.start()
    gc.wait_recv()

    mine_g, other_g = g_out[...], g_in[...]
    gram = dot_high(mine_g, mine_g.T) + dot_high(other_g, other_g.T)
    eye = (
        lax.broadcasted_iota(jnp.int32, (HEAD, HEAD), 0) == lax.broadcasted_iota(jnp.int32, (HEAD, HEAD), 1)
    ).astype(F32)

    def all_sum(a):
        return jnp.sum(jnp.sum(a, axis=1, keepdims=True), axis=0, keepdims=True)

    squares = all_sum(gram * eye)
    gram_squares = all_sum(gram * gram)

    def inverse_root(size):
        shift = 0.1 * squares / size + 1e-06
        norm = jnp.sqrt(gram_squares + 2.0 * shift * squares + size * shift * shift)
        matrix = (gram + shift * eye) / norm
        root = None
        for iteration in range(NEWTON):
            factor = (5.0 * eye - matrix) * 0.25
            root = factor if root is None else dot_high(root, factor)
            if iteration < NEWTON - 1:
                square = dot_high(factor, factor)
                matrix = dot_high(dot_high(square, square), matrix)
        return root

    mixed = dot_high(inverse_root(BLOCK_ROWS), inverse_root(HEAD))
    first = pl.ds(pl.multiple_of(core * 256, 256), 256)
    second = pl.ds(pl.multiple_of((1 - core) * 256, 256), 256)
    p_mine = dot_high(mine_g.T, mixed)
    p_other = dot_high(other_g.T, mixed)
    p_scr[first, :] = p_mine
    p_scr[second, :] = p_other
    mean = (all_sum(p_mine * p_mine) + all_sum(p_other * p_other)) / (BLOCK_ROWS * HEAD)
    own = p_scr[pl.ds(pl.multiple_of((z * 2 + core) * 64, 64), 64), :]
    w_out[...] = (own / jnp.sqrt(mean + 1e-06)).astype(BF16)

    for one in kz + vz + sib + zc + wy + wz + [dq_copy, wc, gc]:
        one.wait_send()

    def finish(t, _):
        for one in ring_copies(t) + sum_copies(t):
            one.wait_send()
        return 0

    lax.fori_loop(0, 7, finish, 0)


def per_device(queries, keys, values, saved_out, grad_out, layer_in):
    vmem = pl.BlockSpec(memory_space=pltpu.VMEM)
    scratch = [
        pltpu.VMEM((Y, Z, 128, HEAD), BF16),
        pltpu.VMEM((Y, Z, 128, HEAD), BF16),
        pltpu.VMEM((ALL_ROWS, HEAD), BF16),
        pltpu.VMEM((ALL_ROWS, HEAD), BF16),
        pltpu.VMEM((ALL_ROWS, HEAD), BF16),
        pltpu.VMEM((HEAD, ALL_ROWS), BF16),
        pltpu.VMEM((HEAD, ALL_ROWS), BF16),
        pltpu.VMEM((8, ALL_ROWS), F32),
        pltpu.VMEM((8, ALL_ROWS), F32),
        pltpu.VMEM((8, ALL_ROWS), F32),
        pltpu.VMEM((8, ALL_ROWS), F32),
        pltpu.VMEM((8, ALL_ROWS), F32),
        pltpu.VMEM((HEAD, ALL_ROWS), F32),
        pltpu.VMEM((CHUNK, HEAD), F32),
        pltpu.VMEM((CHUNK, HEAD), F32),
        pltpu.VMEM((7, CHUNK, HEAD), BF16),
        pltpu.VMEM((7, CHUNK, HEAD), BF16),
        pltpu.VMEM((7, CHUNK, HEAD), BF16),
        pltpu.VMEM((7, CHUNK, HEAD), BF16),
        pltpu.VMEM((3, 128, HEAD), BF16),
        pltpu.VMEM((3, 128, HEAD), BF16),
        pltpu.VMEM((3, 128, HEAD), BF16),
        pltpu.VMEM((3, 128, HEAD), BF16),
        pltpu.VMEM((HEADS, 128, HEAD), F32),
        pltpu.VMEM((HEADS, 128, HEAD), F32),
        pltpu.VMEM((HEADS, 128, HEAD), F32),
        pltpu.VMEM((Y, HEAD, 256), F32),
        pltpu.VMEM((Y, HEAD, 256), F32),
        pltpu.VMEM((Y, HEAD, 256), F32),
        pltpu.VMEM((7, HEAD, 256), BF16),
        pltpu.VMEM((7, HEAD, 256), BF16),
        pltpu.VMEM((HEAD, 256), BF16),
        pltpu.VMEM((3, HEAD, 256), BF16),
        pltpu.VMEM((HEAD, 256), F32),
        pltpu.VMEM((HEAD, 256), F32),
        pltpu.VMEM((BLOCK_ROWS, HEAD), F32),
        pltpu.SemaphoreType.DMA((N_SEMS,)),
        pltpu.SemaphoreType.DMA((N_SEMS,)),
    ]
    shapes = (
        jax.ShapeDtypeStruct(queries.shape, BF16),
        jax.ShapeDtypeStruct(keys.shape, BF16),
        jax.ShapeDtypeStruct(values.shape, BF16),
        jax.ShapeDtypeStruct((64, HEAD), BF16),
    )
    return pl.pallas_call(
        kernel,
        out_shape=shapes,
        in_specs=[vmem] * 6,
        out_specs=(vmem,) * 4,
        scratch_shapes=scratch,
        compiler_params=pltpu.CompilerParams(
            collective_id=0, has_side_effects=True, vmem_limit_bytes=50 * 1024 * 1024
        ),
    )(queries, keys, values, saved_out, grad_out, layer_in)


def solution(mesh):
    placed = (P("ctx", "tp"),) * 5 + (P("ctx", None),)
    return jax.shard_map(
        per_device,
        mesh=mesh,
        in_specs=placed,
        out_specs=(P("ctx", "tp"),) * 4,
        check_vma=False,
    )
```

time: 1070 us -> 126 us (0.12)
  waiting for transfers between devices: 800 us -> 0 us
  blocking collectives: 192 us -> 0 us
  Pallas kernels: 0 us -> 117 us
  matrix products: 26.2 us -> 0 us
  starting transfers between devices: 17.6 us -> 0 us
  between operations: 17.4 us -> 0.66 us
    psum x1 -> x0, waiting for transfers between devices: 522 us -> none  [weight_block(): weight_gradient = lax.psum(local_term, 'ctx')]
    all_to_all x1 -> x0, blocking collectives: 192 us -> none  [per_device(): lax.all_to_all(value_parts, 'ctx', split_axis=0, concat_axis=0, tiled=True)]
    all_gather x2 -> x0, waiting for transfers between devices: 173 us -> none  [the longest x1 90.1 us: per_device(): lax.all_gather(keys, 'ctx', axis=0, tiled=True)]
    pallas_call x0 -> x1, Pallas kernels: none -> 117 us  [per_device(): pl.pallas_call(kernel, out_shape=shapes, in_specs=[vmem] * 6, out_specs=(...]
    all_to_all x1 -> x0, waiting for transfers between devices: 102 us -> none  [per_device(): lax.all_to_all(key_parts, 'ctx', split_axis=0, concat_axis=0, tiled=True)]
    dot_general x21 -> x0, matrix products: 26.2 us -> none  [the longest x14 17.6 us: matmul_high(): return jnp.matmul(first_mat, second_mat, precision=highest)]
    all_to_all x1 -> x0, starting transfers between devices: 17.3 us -> none  [per_device(): lax.all_to_all(key_parts, 'ctx', split_axis=0, concat_axis=0, tiled=True)]
  transfers between devices with their start and end apart: 4 -> 0, of which waited for: 4 -> 0; matrix products, arithmetic and copies ran while one was open for 1% -> 0% of each run, Pallas kernels for 0% -> 0%
where the time goes in v1:
time: 126 us
  Pallas kernels  117 us (93%)
  local copies, waits for them, and re-layouts  7.93 us (6%)
    pallas_call x1, Pallas kernels, per_device(): pl.pallas_call(kernel, out_shape=shapes, in_specs=[vmem] * 6, out_specs=(...  117 us
    unnamed x16, local copies, waits for them, and re-layouts  7.93 us

profile of v1, /device:TPU:1, one launch (start us, length us, event | category | flops | bytes accessed | tf_op | source)
XLA Modules:
  0.0 126.0 jit_solution(13346748255636846132)
XLA Ops:
  0.6 0.0 copy-start
  0.6 1.2 copy-done
  1.9 0.0 copy-start.1
  1.9 0.9 copy-done.1
  2.8 0.0 copy-start.2
  2.8 0.9 copy-done.2
  3.7 0.0 copy-start.3
  3.7 0.9 copy-done.3
  4.6 0.0 copy-start.4
  4.6 0.8 copy-done.4
  5.3 0.0 copy-start.5
  5.3 0.8 copy-done.5
  6.1 117.4 %shard_map.93 = (bf16[128,512]{1,0:T(8,128)(2,1)S(1)}, bf16[128,128]{1,0:T(8,128)(2,1)S(1)}, bf16[128,128]{1,0:T(8,128)(2,1)S(1)}, bf16[64,128]{1,0:T(8,128)(2,1)S(1)}) custom-call(bf16[128,512]{1,0:T(8,128)(2,1)S(1)} %copy-done.1, bf16[128,128]{1,0:T(8,128)(2,1)S(1)} %copy-done.4, bf16[128,128]{1,0:T(8,128)(2,1)S(1)} %copy-done.5, ...), custom_call_target="tpu_custom_call" | custom-call | tf_op jit(solution)/shard_map/pallas_call | solution.py:420
  123.5 0.7 copy.14
  124.2 0.6 copy.15
  124.8 0.6 copy.16
  125.4 0.6 copy.17
Async XLA Ops:
  0.6 1.2 copy-start
  1.9 0.9 copy-start.1
  2.8 0.9 copy-start.2
  3.7 0.9 copy-start.3
  4.6 0.8 copy-start.4
  5.3 0.8 copy-start.5

commit v2 on v1

v2 whole, which is shorter than its diff:
```python
import jax
import jax.numpy as jnp
from jax import lax
from jax.experimental import pallas as pl
from jax.experimental.pallas import tpu as pltpu
from jax.sharding import PartitionSpec as P

HEAD = 128
Y, Z = 8, 4
HEADS = 4
KEYS = 1024
NEWTON = 2
BLOCK_ROWS = 512
FILL = -1e30
SCALE = HEAD ** (-0.5)
SCALE2 = SCALE * 1.4426950408889634
HIGHEST = lax.Precision.HIGHEST
F32 = jnp.float32
BF16 = jnp.bfloat16
NT = (((1,), (1,)), ((), ()))

GROUPS = dict(
    KZ=3, VZ=3, KC=4, VC=4, RQ=7, RD=7, ST=7, XZ=3, DVC=1, ZV=3, VG=3, WC=1, WY=7, WZ=3, GC=1, RS=7, DKC=1, ZK=3
)
BASE, N_SEMS = {}, 0
for _name, _count in GROUPS.items():
    BASE[_name] = N_SEMS
    N_SEMS += _count


def dot(a, b, dims=(((1,), (0,)), ((), ())), precision=None):
    return lax.dot_general(a, b, dims, precision=precision, preferred_element_type=F32)


def dot_high(a, b, dims=(((1,), (0,)), ((), ()))):
    return dot(a, b, dims, precision=HIGHEST)


def kernel(
    q_ref, k_ref, v_ref, o_ref, do_ref, x_ref,
    dq_out, dk_out, dv_out, w_out,
    qs, dos, obuf, kl, vl, kt, xin, xs, xw, ptil,
    tops, stat, stat_in, factor, delta, dv_acc, dk_acc, tmp_q, out_q, in_q,
    dv_send, dv_in, dk_send, dk_in, zout_v, zin_v, zout_k, zin_k, vg,
    w_full, w_in, wk, wy_out, wy_in, gbuf, gbuf_in, gt, p_scr,
    send, recv, load,
):
    c = lax.axis_index("ctx")
    core = lax.rem(c, 2)
    z = lax.rem(c // 2, Z)
    y = c // (2 * Z)
    block = z * 2 + core

    def dev(yy, zz, cc):
        return {"ctx": (yy * Z + zz) * 2 + cc}

    sibling = dev(y, z, 1 - core)

    def at_y(step):
        return lax.rem(y + step + Y, Y)

    def at_z(step):
        return lax.rem(z + step, Z)

    def rows_of(number, size):
        return pl.ds(pl.multiple_of(number * size, size), size)

    sent = []

    def copy(src, dst, group, number, device):
        return pltpu.make_async_remote_copy(
            src_ref=src, dst_ref=dst, send_sem=send.at[BASE[group] + number], recv_sem=recv.at[BASE[group] + number],
            device_id=device, device_id_type=pl.DeviceIdType.MESH,
        )

    def start(copies):
        for one in copies:
            one.start()
            sent.append(one)
        return copies

    def wait_recv(copies):
        for one in copies:
            one.wait_recv()

    heads = [pl.ds(h * HEAD, HEAD) for h in range(HEADS)]
    pairs = [(k_ref, kl.at[rows_of(block, 128)])]
    pairs += [(q_ref.at[:, heads[h]], qs.at[y, h]) for h in range(HEADS)]
    pairs += [(do_ref.at[:, heads[h]], dos.at[y, h]) for h in range(HEADS)]
    pairs += [(v_ref, vl.at[rows_of(block, 128)])]
    pairs += [(o_ref.at[:, heads[h]], obuf.at[h]) for h in range(HEADS)]
    pairs += [(x_ref, xin)]
    loads = [pltpu.make_async_copy(src, dst, load.at[n]) for n, (src, dst) in enumerate(pairs)]
    for one in loads:
        one.start()

    barrier = pltpu.get_barrier_semaphore()
    partners = [dev(at_y(i), z, core) for i in range(1, Y)]
    partners += [dev(y, at_z(i), core) for i in range(1, Z)] + [sibling]
    for partner in partners:
        pl.semaphore_signal(barrier, inc=1, device_id=partner, device_id_type=pl.DeviceIdType.MESH)
    for one in loads[:5]:
        one.wait()
    pl.semaphore_wait(barrier, len(partners))

    def ring_target(t):
        return dev(jnp.where(lax.rem(t, 2) == 0, at_y(1), at_y(-1)), z, core)

    def ring_copy(buf, group, t):
        chunk = jnp.where(lax.rem(t, 2) == 0, at_y(-(t // 2)), at_y(t // 2))
        return copy(buf.at[chunk], buf.at[chunk], group, t, ring_target(t))

    def ring_arrival(t):
        return jnp.where(lax.rem(t, 2) == 0, at_y(-1 - t // 2), at_y(1 + t // 2))

    def ring_wait(buf, group, t):
        chunk = ring_arrival(t)
        copy(buf.at[chunk], buf.at[chunk], group, t, sibling).wait_recv()

    def block_copies(buf, group):
        mine = buf.at[rows_of(block, 128)]
        return [copy(mine, mine, group, i - 1, dev(y, at_z(i), core)) for i in range(1, Z)]

    def core_copy(buf, group, i):
        rows = rows_of(at_z(i) * 2 + core, 128)
        return copy(buf.at[rows], buf.at[rows], group, i, sibling)

    def arrived_block(buf, group, i):
        rows = rows_of(at_z(Z - i) * 2 + core, 128)
        copy(buf.at[rows], buf.at[rows], group, i - 1, sibling).wait_recv()

    def core_wait(buf, group, i):
        rows = rows_of(at_z(i) * 2 + 1 - core, 128)
        copy(buf.at[rows], buf.at[rows], group, i, sibling).wait_recv()

    start(block_copies(kl, "KZ"))
    for t in range(2):
        ring_copy(qs, "RQ", t).start()
    start([core_copy(kl, "KC", 0)])
    for one in loads[5:]:
        one.wait()
    start(block_copies(vl, "VZ"))
    start([core_copy(vl, "VC", 0)])

    stat[...] = jnp.full(stat.shape, FILL, F32)
    tops[...] = jnp.full(tops.shape, FILL, F32)
    dv_acc[...] = jnp.zeros(dv_acc.shape, F32)
    dk_acc[...] = jnp.zeros(dk_acc.shape, F32)
    for h in range(HEADS):
        product = dos[y, h].astype(F32) * obuf[h].astype(F32)
        stat[8:9, h * HEAD : (h + 1) * HEAD] = jnp.sum(product.T, axis=0, keepdims=True)

    def arrange(i, _):
        for zz in range(Z):
            xs[zz, :, rows_of(i, 128)] = xin[:, rows_of(i * Z + zz, 128)]
        return 0

    lax.fori_loop(0, Y, arrange, 0)

    for i in range(1, Z):
        arrived_block(kl, "KZ", i)
        start([core_copy(kl, "KC", Z - i)])
    for i in range(Z):
        core_wait(kl, "KC", i)

    def row_of(ref, chunk, cols):
        number = lax.broadcasted_iota(jnp.int32, (Y, 256), 0)
        return jnp.sum(jnp.where(number == chunk, ref[0:Y, cols], 0.0), axis=0, keepdims=True)

    def put_row(ref, chunk, cols, row):
        number = lax.broadcasted_iota(jnp.int32, (Y, 256), 0)
        ref[0:Y, cols] = jnp.where(number == chunk, row, ref[0:Y, cols])

    halves = [slice(0, 256), slice(256, 512)]

    def forward(chunk, diagonal):
        for n, cols in enumerate(halves):
            q2 = qs[chunk, 2 * n : 2 * n + 2].reshape(256, HEAD)
            s = dot(kl[...], q2, NT) * SCALE2
            if diagonal:
                key = lax.broadcasted_iota(jnp.int32, (KEYS, 256), 0)
                row = (lax.broadcasted_iota(jnp.int32, (KEYS, 256), 1) & 127) + block * 128
                s = jnp.where(key <= row, s, FILL)
            top = jnp.max(s, axis=0, keepdims=True)
            e = jnp.exp2(s - top)
            ptil[chunk, n] = e
            put_row(tops, chunk, cols, top)
            put_row(stat, chunk, cols, top + jnp.log2(jnp.sum(e, axis=0, keepdims=True)))

    def gather_step(t, _):
        @pl.when(t >= 2)
        def _():
            ring_wait(qs, "RQ", t - 2)
            ring_copy(qs, "RQ", t).start()

        @pl.when(t == 1)
        def _():
            forward(y, True)

        @pl.when(t >= 2)
        def _():
            chunk = ring_arrival(t - 2)

            @pl.when(chunk > y)
            def _():
                forward(chunk, False)

        return 0

    lax.fori_loop(1, 7, gather_step, 0)
    for t in range(2):
        ring_copy(dos, "RD", t).start()
    xz = start([copy(xs.at[at_z(i)], xw.at[z], "XZ", i - 1, dev(y, at_z(i), core)) for i in range(1, Z)])
    xw[z] = xs[z]
    for i in range(1, Z):
        arrived_block(vl, "VZ", i)
        start([core_copy(vl, "VC", Z - i)])

    def gather_end(t, _):
        ring_wait(qs, "RQ", t)
        chunk = ring_arrival(t)

        @pl.when(chunk > y)
        def _():
            forward(chunk, False)

        return 0

    lax.fori_loop(5, 7, gather_end, 0)

    st = start([copy(stat, stat_in.at[i - 1], "ST", i - 1, dev(at_y(i), z, core)) for i in range(1, Y)])
    for t in range(2):
        ring_wait(dos, "RD", t)
        ring_copy(dos, "RD", t + 2).start()
    kt[...] = kl[...].astype(F32).T.astype(BF16)
    wait_recv(st)
    parts = [stat[0:8, :]] + [stat_in[i, 0:8, :] for i in range(Y - 1)]
    high = parts[0]
    for part in parts[1:]:
        high = jnp.maximum(high, part)
    total = sum(jnp.exp2(part - high) for part in parts)
    factor[...] = jnp.exp2(tops[...] - (high + jnp.log2(total)))
    number = lax.broadcasted_iota(jnp.int32, (Y, 512), 0)
    all_delta = jnp.where(number == y, stat[8:9, :], 0.0)
    for i in range(1, Y):
        all_delta = jnp.where(number == at_y(Y - i), stat_in[i - 1, 8:9, :], all_delta)
    delta[...] = all_delta

    def value_tile(chunk):
        for n, cols in enumerate(halves):
            p = (ptil[chunk, n] * row_of(factor, chunk, cols)).astype(BF16)
            dv_acc[...] += dot(p, dos[chunk, 2 * n : 2 * n + 2].reshape(256, HEAD))

    def value_step(n, _):
        t = jnp.maximum(n - 1, 0)

        @pl.when(n >= 3)
        def _():
            ring_wait(dos, "RD", t)

        @pl.when(jnp.logical_and(n >= 3, n < 6))
        def _():
            ring_copy(dos, "RD", t + 2).start()

        chunk = jnp.where(n == 0, y, ring_arrival(t))

        @pl.when(chunk >= y)
        def _():
            value_tile(chunk)

        return 0

    lax.fori_loop(0, 8, value_step, 0)

    def split_cores(acc, out):
        for zz in range(Z):
            out[zz] = acc[rows_of(zz * 2 + 1 - core, 128), :]

    def z_sums(acc, got, out, into, group):
        copies = []
        for i in range(1, Z):
            zz = at_z(i)
            out[i - 1] = (acc[rows_of(zz * 2 + core, 128), :] + got[zz]).astype(BF16)
            copies.append(copy(out.at[i - 1], into.at[i - 1], group, i - 1, dev(y, zz, core)))
        return copies

    def z_total(acc, got, into):
        total = acc[rows_of(block, 128), :] + got[z]
        for i in range(Z - 1):
            total = total + into[i].astype(F32)
        return total.astype(BF16)

    split_cores(dv_acc, dv_send)
    dvc = start([copy(dv_send, dv_in, "DVC", 0, sibling)])

    zv = [copy(zout_v.at[i - 1], zin_v.at[i - 1], "ZV", i - 1, dev(y, at_z(i), core)) for i in range(1, Z)]
    vgc = [copy(vg.at[z], vg.at[z], "VG", i - 1, dev(y, at_z(i), core)) for i in range(1, Z)]
    wc = [copy(w_full.at[rows_of(1 - core, 64)], w_in, "WC", 0, sibling)]
    wy = [copy(wy_out.at[i - 1], wy_in.at[i - 1], "WY", i - 1, dev(at_y(i), z, core)) for i in range(1, Y)]

    def chain_1():
        wait_recv(dvc)
        z_sums(dv_acc, dv_in, zout_v, zin_v, "ZV")
        start(zv)

    def chain_2():
        wait_recv(zv)
        vg[z] = z_total(dv_acc, dv_in, zin_v)
        start(vgc)
        dv_out[...] = vg[z]

    def chain_3():
        wait_recv(vgc)
        wait_recv(xz)
        value_t = vg[...].reshape(512, HEAD).astype(F32).T.astype(BF16)
        for n in range(4):
            cols = slice(n * 256, (n + 1) * 256)
            w_full[:, cols] = dot(value_t, xw[:, :, cols].reshape(512, 256))
        start(wc)

    def chain_4():
        wait_recv(wc)
        kept = w_full[rows_of(core, 64), :] + w_in[...]
        for i in range(Y):
            wk[i] = kept[:, i * 128 : (i + 1) * 128]
        for i in range(1, Y):
            wy_out[i - 1] = wk[at_y(i)].astype(BF16)
        start(wy)

    def tile(chunk):
        for n, cols in enumerate(halves):
            q2 = qs[chunk, 2 * n : 2 * n + 2].reshape(256, HEAD)
            do2 = dos[chunk, 2 * n : 2 * n + 2].reshape(256, HEAD)
            p = ptil[chunk, n] * row_of(factor, chunk, cols)
            dp = dot(vl[...], do2, NT)
            ds = (p * (dp - row_of(delta, chunk, cols)) * SCALE).astype(BF16)
            dk_acc[...] += dot(ds, q2)
            tmp_q[:, cols] = dot(kt[...], ds)

    def sum_copy(t):
        return copy(out_q.at[t], in_q.at[t], "RS", t, ring_target(t))

    for i in range(Z):
        core_wait(vl, "VC", i)

    def tile_step(t, _):
        s = t // 2
        chunk = jnp.where(t == 7, y, jnp.where(lax.rem(t, 2) == 0, at_y(4 - s), at_y(s - 3)))

        @pl.when(chunk >= y)
        def _():
            tile(chunk)

        @pl.when(chunk < y)
        def _():
            tmp_q[...] = jnp.zeros(tmp_q.shape, F32)

        @pl.when(jnp.logical_and(t >= 2, t < 7))
        def _():
            sum_copy(t - 2).wait_recv()
            tmp_q[...] += in_q[t - 2].astype(F32)

        @pl.when(t < 7)
        def _():
            out_q[t] = tmp_q[...].astype(BF16)
            sum_copy(t).start()

        for when, chain in ((0, chain_1), (2, chain_2), (4, chain_3), (5, chain_4)):
            pl.when(t == when)(chain)
        return 0

    lax.fori_loop(0, 8, tile_step, 0)

    split_cores(dk_acc, dk_send)
    dkc = start([copy(dk_send, dk_in, "DKC", 0, sibling)])

    wait_recv(wy)
    g = wk[y]
    for i in range(Y - 1):
        g = g + wy_in[i].astype(F32)
    gbuf[z] = g
    wz = start([copy(gbuf.at[z], gbuf.at[z], "WZ", i - 1, dev(y, at_z(i), core)) for i in range(1, Z)])

    wait_recv(dkc)
    zk = start(z_sums(dk_acc, dk_in, zout_k, zin_k, "ZK"))

    wait_recv(wz)
    gc = start([copy(gbuf, gbuf_in, "GC", 0, sibling)])

    for t in (5, 6):
        sum_copy(t).wait_recv()
    tmp_q[...] += in_q[5].astype(F32) + in_q[6].astype(F32)
    for h in range(HEADS):
        dq_out[:, h * HEAD : (h + 1) * HEAD] = tmp_q[:, h * HEAD : (h + 1) * HEAD].T.astype(BF16)

    wait_recv(gc)
    for zz in range(Z):
        gt[rows_of(core, 64), zz * 128 : (zz + 1) * 128] = gbuf[zz]
        gt[rows_of(1 - core, 64), zz * 128 : (zz + 1) * 128] = gbuf_in[zz]

    grad_t = gt[...]
    gram = dot_high(grad_t, grad_t, NT)
    eye = (
        lax.broadcasted_iota(jnp.int32, (HEAD, HEAD), 0) == lax.broadcasted_iota(jnp.int32, (HEAD, HEAD), 1)
    ).astype(F32)

    def all_sum(a):
        return jnp.sum(jnp.sum(a, axis=0, keepdims=True), axis=1, keepdims=True)

    squares = all_sum(gram * eye)
    gram_squares = all_sum(gram * gram)

    def inverse_root(size):
        shift = 0.1 * squares / size + 1e-06
        norm = jnp.sqrt(gram_squares + 2.0 * shift * squares + size * shift * shift)
        matrix = (gram + shift * eye) / norm
        root = None
        for iteration in range(NEWTON):
            part = (5.0 * eye - matrix) * 0.25
            root = part if root is None else dot_high(root, part)
            if iteration < NEWTON - 1:
                square = dot_high(part, part)
                matrix = dot_high(dot_high(square, square), matrix)
        return root

    mixed = dot_high(inverse_root(BLOCK_ROWS), inverse_root(HEAD))
    precond_t = dot_high(mixed, grad_t)
    mean = all_sum(precond_t * precond_t) / (BLOCK_ROWS * HEAD)
    p_scr[...] = (precond_t / jnp.sqrt(mean + 1e-06)).T
    w_out[...] = p_scr[rows_of(block, 64), :].astype(BF16)

    wait_recv(zk)
    dk_out[...] = z_total(dk_acc, dk_in, zin_k)

    for one in sent:
        one.wait_send()

    def finish(t, _):
        for one in (ring_copy(qs, "RQ", t), ring_copy(dos, "RD", t), sum_copy(t)):
            one.wait_send()
        return 0

    lax.fori_loop(0, 7, finish, 0)


def per_device(queries, keys, values, saved_out, grad_out, layer_in):
    vmem = pl.BlockSpec(memory_space=pltpu.VMEM)
    hbm = pl.BlockSpec(memory_space=pl.ANY)
    row_chunk = (HEADS, 128, HEAD)
    scratch = [
        pltpu.VMEM((Y,) + row_chunk, BF16),
        pltpu.VMEM((Y,) + row_chunk, BF16),
        pltpu.VMEM(row_chunk, BF16),
        pltpu.VMEM((KEYS, HEAD), BF16),
        pltpu.VMEM((KEYS, HEAD), BF16),
        pltpu.VMEM((HEAD, KEYS), BF16),
        pltpu.VMEM((128, 4096), BF16),
        pltpu.VMEM((Z, 128, 1024), BF16),
        pltpu.VMEM((Z, 128, 1024), BF16),
        pltpu.VMEM((Y, 2, KEYS, 256), F32),
        pltpu.VMEM((Y, 512), F32),
        pltpu.VMEM((16, 512), F32),
        pltpu.VMEM((Y - 1, 16, 512), F32),
        pltpu.VMEM((Y, 512), F32),
        pltpu.VMEM((Y, 512), F32),
        pltpu.VMEM((KEYS, HEAD), F32),
        pltpu.VMEM((KEYS, HEAD), F32),
        pltpu.VMEM((HEAD, 512), F32),
        pltpu.VMEM((7, HEAD, 512), BF16),
        pltpu.VMEM((7, HEAD, 512), BF16),
        pltpu.VMEM((Z, 128, HEAD), F32),
        pltpu.VMEM((Z, 128, HEAD), F32),
        pltpu.VMEM((Z, 128, HEAD), F32),
        pltpu.VMEM((Z, 128, HEAD), F32),
        pltpu.VMEM((3, 128, HEAD), BF16),
        pltpu.VMEM((3, 128, HEAD), BF16),
        pltpu.VMEM((3, 128, HEAD), BF16),
        pltpu.VMEM((3, 128, HEAD), BF16),
        pltpu.VMEM((Z, 128, HEAD), BF16),
        pltpu.VMEM((HEAD, 1024), F32),
        pltpu.VMEM((64, 1024), F32),
        pltpu.VMEM((Y, 64, 128), F32),
        pltpu.VMEM((7, 64, 128), BF16),
        pltpu.VMEM((7, 64, 128), BF16),
        pltpu.VMEM((Z, 64, 128), F32),
        pltpu.VMEM((Z, 64, 128), F32),
        pltpu.VMEM((HEAD, BLOCK_ROWS), F32),
        pltpu.VMEM((BLOCK_ROWS, HEAD), F32),
        pltpu.SemaphoreType.DMA((N_SEMS,)),
        pltpu.SemaphoreType.DMA((N_SEMS,)),
        pltpu.SemaphoreType.DMA((15,)),
    ]
    shapes = (
        jax.ShapeDtypeStruct(queries.shape, BF16),
        jax.ShapeDtypeStruct(keys.shape, BF16),
        jax.ShapeDtypeStruct(values.shape, BF16),
        jax.ShapeDtypeStruct((64, HEAD), BF16),
    )
    return pl.pallas_call(
        kernel,
        out_shape=shapes,
        in_specs=[hbm] * 6,
        out_specs=(vmem,) * 4,
        scratch_shapes=scratch,
        compiler_params=pltpu.CompilerParams(
            collective_id=0, has_side_effects=True, vmem_limit_bytes=60 * 1024 * 1024
        ),
    )(queries, keys, values, saved_out, grad_out, layer_in)


def solution(mesh):
    placed = (P("ctx", "tp"),) * 5 + (P("ctx", None),)
    return jax.shard_map(
        per_device,
        mesh=mesh,
        in_specs=placed,
        out_specs=(P("ctx", "tp"),) * 4,
        check_vma=False,
    )
```

time: 126 us -> 97.5 us (0.77)
  Pallas kernels: 117 us -> 92.9 us
  local copies, waits for them, and re-layouts: 7.93 us -> 3.68 us
    pallas_call x1, Pallas kernels: 117 us -> 92.9 us  [per_device(): pl.pallas_call(kernel, out_shape=shapes, in_specs=[hbm] * 6, out_specs=(v...]
    unnamed x16 -> x10, local copies, waits for them, and re-layouts: 7.93 us -> 3.68 us
where the time goes in v2:
time: 97.5 us; the launch traced here: 97.2 us
  Pallas kernels  92.9 us (95%)
  local copies, waits for them, and re-layouts  3.68 us (4%)
    pallas_call x1, Pallas kernels, per_device(): pl.pallas_call(kernel, out_shape=shapes, in_specs=[hbm] * 6, out_specs=(v...  92.9 us
    unnamed x10, local copies, waits for them, and re-layouts  3.68 us

profile of v2, /device:TPU:1, one launch (start us, length us, event | category | flops | bytes accessed | tf_op | source)
XLA Modules:
  0.0 97.2 jit_solution(1530381469070341708)
XLA Ops:
  0.6 92.9 %shard_map.93 = (bf16[128,512]{1,0:T(8,128)(2,1)}, bf16[128,128]{1,0:T(8,128)(2,1)}, bf16[128,128]{1,0:T(8,128)(2,1)}, bf16[64,128]{1,0:T(8,128)(2,1)}) custom-call(bf16[128,512]{1,0:T(8,128)(2,1)} %q_ref.1, bf16[128,128]{1,0:T(8,128)(2,1)} %k_ref.1, bf16[128,128]{1,0:T(8,128)(2,1)} %v_ref.1, bf16[128,512]{1,0:T(8,128)(2,1)} %o_ref.1, ...), custom_call_target="tpu_custom_call" | custom-call | tf_op jit(solution)/shard_map/pallas_call | solution.py:499
  93.6 0.0 copy-start.1
  93.6 1.6 %copy.14 = bf16[128,512]{1,0:T(8,128)(2,1)} copy(bf16[128,512]{1,0:T(8,128)(2,1)} %get-tuple-element.8) | data formatting | bytes 262144
  95.1 0.0 copy-done.1
  95.1 0.0 copy-start
  95.1 0.6 copy.15
  95.8 0.2 copy-done
  95.9 0.0 copy-start.2
  95.9 0.6 copy.16
  96.5 0.1 copy-done.2
  96.6 0.6 copy.17
Async XLA Ops:
  93.6 1.6 %copy-start.1 = (bf16[128,128]{1,0:T(8,128)(2,1)S(1)}, bf16[128,128]{1,0:T(8,128)(2,1)}, u32[]{:S(2)}) copy-start(bf16[128,128]{1,0:T(8,128)(2,1)} %get-tuple-element.9) | copy-start | bytes 98308
  95.1 0.8 copy-start
  95.9 0.7 copy-start.2

commit v3 on v2

--- a/solution.py
+++ b/solution.py
@@ -137,7 +137,11 @@
     for t in range(2):
         ring_copy(qs, "RQ", t).start()
     start([core_copy(kl, "KC", 0)])
-    for one in loads[5:]:
+    for one in loads[5:9]:
+        one.wait()
+    for t in range(2):
+        ring_copy(dos, "RD", t).start()
+    for one in loads[9:]:
         one.wait()
     start(block_copies(vl, "VZ"))
     start([core_copy(vl, "VC", 0)])
@@ -160,8 +164,6 @@
     for i in range(1, Z):
         arrived_block(kl, "KZ", i)
         start([core_copy(kl, "KC", Z - i)])
-    for i in range(Z):
-        core_wait(kl, "KC", i)
 
     def row_of(ref, chunk, cols):
         number = lax.broadcasted_iota(jnp.int32, (Y, 256), 0)
@@ -187,51 +189,60 @@
             put_row(tops, chunk, cols, top)
             put_row(stat, chunk, cols, top + jnp.log2(jnp.sum(e, axis=0, keepdims=True)))
 
-    def gather_step(t, _):
-        @pl.when(t >= 2)
-        def _():
-            ring_wait(qs, "RQ", t - 2)
-            ring_copy(qs, "RQ", t).start()
-
-        @pl.when(t == 1)
-        def _():
+    def pass_on(buf, group, t):
+        ring_wait(buf, group, t)
+
+        @pl.when(t + 1 < 7)
+        def _():
+            ring_wait(buf, group, t + 1)
+
+        @pl.when(t + 2 < 7)
+        def _():
+            ring_copy(buf, group, t + 2).start()
+
+        @pl.when(t + 3 < 7)
+        def _():
+            ring_copy(buf, group, t + 3).start()
+
+    def gather_step(n, _):
+        t = jnp.maximum(n - 1, 0)
+
+        @pl.when(jnp.logical_or(n == 0, jnp.logical_and(n > 1, lax.rem(t, 2) == 0)))
+        def _():
+            pass_on(qs, "RQ", t)
+
+        @pl.when(n == 0)
+        def _():
+            for i in range(Z):
+                core_wait(kl, "KC", i)
             forward(y, True)
 
-        @pl.when(t >= 2)
-        def _():
-            chunk = ring_arrival(t - 2)
-
-            @pl.when(chunk > y)
-            def _():
-                forward(chunk, False)
+        @pl.when(jnp.logical_or(n == 0, jnp.logical_and(n > 2, lax.rem(n, 2) == 0)))
+        def _():
+            pass_on(dos, "RD", jnp.maximum(n - 2, 0))
+
+        @pl.when(n == 2)
+        def _():
+            for i in range(1, Z):
+                arrived_block(vl, "VZ", i)
+                start([vc[Z - i]])
+            start(xz)
+
+        chunk = ring_arrival(t)
+
+        @pl.when(jnp.logical_and(n > 0, chunk > y))
+        def _():
+            forward(chunk, False)
 
         return 0
 
-    lax.fori_loop(1, 7, gather_step, 0)
-    for t in range(2):
-        ring_copy(dos, "RD", t).start()
-    xz = start([copy(xs.at[at_z(i)], xw.at[z], "XZ", i - 1, dev(y, at_z(i), core)) for i in range(1, Z)])
+    xz = [copy(xs.at[at_z(i)], xw.at[z], "XZ", i - 1, dev(y, at_z(i), core)) for i in range(1, Z)]
     xw[z] = xs[z]
-    for i in range(1, Z):
-        arrived_block(vl, "VZ", i)
-        start([core_copy(vl, "VC", Z - i)])
-
-    def gather_end(t, _):
-        ring_wait(qs, "RQ", t)
-        chunk = ring_arrival(t)
-
-        @pl.when(chunk > y)
-        def _():
-            forward(chunk, False)
-
-        return 0
-
-    lax.fori_loop(5, 7, gather_end, 0)
+    vc = [core_copy(vl, "VC", i) for i in range(Z)]
+    lax.fori_loop(0, 8, gather_step, 0)
 
     st = start([copy(stat, stat_in.at[i - 1], "ST", i - 1, dev(at_y(i), z, core)) for i in range(1, Y)])
-    for t in range(2):
-        ring_wait(dos, "RD", t)
-        ring_copy(dos, "RD", t + 2).start()
+    ring_wait(dos, "RD", 6)
     kt[...] = kl[...].astype(F32).T.astype(BF16)
     wait_recv(st)
     parts = [stat[0:8, :]] + [stat_in[i, 0:8, :] for i in range(Y - 1)]
@@ -252,17 +263,7 @@
             dv_acc[...] += dot(p, dos[chunk, 2 * n : 2 * n + 2].reshape(256, HEAD))
 
     def value_step(n, _):
-        t = jnp.maximum(n - 1, 0)
-
-        @pl.when(n >= 3)
-        def _():
-            ring_wait(dos, "RD", t)
-
-        @pl.when(jnp.logical_and(n >= 3, n < 6))
-        def _():
-            ring_copy(dos, "RD", t + 2).start()
-
-        chunk = jnp.where(n == 0, y, ring_arrival(t))
+        chunk = jnp.where(n == 0, y, ring_arrival(jnp.maximum(n - 1, 0)))
 
         @pl.when(chunk >= y)
         def _():
@@ -297,6 +298,9 @@
     vgc = [copy(vg.at[z], vg.at[z], "VG", i - 1, dev(y, at_z(i), core)) for i in range(1, Z)]
     wc = [copy(w_full.at[rows_of(1 - core, 64)], w_in, "WC", 0, sibling)]
     wy = [copy(wy_out.at[i - 1], wy_in.at[i - 1], "WY", i - 1, dev(at_y(i), z, core)) for i in range(1, Y)]
+
+    wz = [copy(gbuf.at[z], gbuf.at[z], "WZ", i - 1, dev(y, at_z(i), core)) for i in range(1, Z)]
+    gc = [copy(gbuf, gbuf_in, "GC", 0, sibling)]
 
     def chain_1():
         wait_recv(dvc)
@@ -326,6 +330,18 @@
         for i in range(1, Y):
             wy_out[i - 1] = wk[at_y(i)].astype(BF16)
         start(wy)
+
+    def chain_5():
+        wait_recv(wy)
+        g = wk[y]
+        for i in range(Y - 1):
+            g = g + wy_in[i].astype(F32)
+        gbuf[z] = g
+        start(wz)
+
+    def chain_6():
+        wait_recv(wz)
+        start(gc)
 
     def tile(chunk):
         for n, cols in enumerate(halves):
@@ -355,6 +371,9 @@
         def _():
             tmp_q[...] = jnp.zeros(tmp_q.shape, F32)
 
+        for when, chain in ((2, chain_2), (4, chain_4), (6, chain_5)):
+            pl.when(t == when)(chain)
+
         @pl.when(jnp.logical_and(t >= 2, t < 7))
         def _():
             sum_copy(t - 2).wait_recv()
@@ -365,7 +384,7 @@
             out_q[t] = tmp_q[...].astype(BF16)
             sum_copy(t).start()
 
-        for when, chain in ((0, chain_1), (2, chain_2), (4, chain_3), (5, chain_4)):
+        for when, chain in ((0, chain_1), (3, chain_3), (7, chain_6)):
             pl.when(t == when)(chain)
         return 0
 
@@ -373,25 +392,8 @@
 
     split_cores(dk_acc, dk_send)
     dkc = start([copy(dk_send, dk_in, "DKC", 0, sibling)])
-
-    wait_recv(wy)
-    g = wk[y]
-    for i in range(Y - 1):
-        g = g + wy_in[i].astype(F32)
-    gbuf[z] = g
-    wz = start([copy(gbuf.at[z], gbuf.at[z], "WZ", i - 1, dev(y, at_z(i), core)) for i in range(1, Z)])
-
     wait_recv(dkc)
     zk = start(z_sums(dk_acc, dk_in, zout_k, zin_k, "ZK"))
-
-    wait_recv(wz)
-    gc = start([copy(gbuf, gbuf_in, "GC", 0, sibling)])
-
-    for t in (5, 6):
-        sum_copy(t).wait_recv()
-    tmp_q[...] += in_q[5].astype(F32) + in_q[6].astype(F32)
-    for h in range(HEADS):
-        dq_out[:, h * HEAD : (h + 1) * HEAD] = tmp_q[:, h * HEAD : (h + 1) * HEAD].T.astype(BF16)
 
     wait_recv(gc)
     for zz in range(Z):
@@ -428,6 +430,12 @@
     mean = all_sum(precond_t * precond_t) / (BLOCK_ROWS * HEAD)
     p_scr[...] = (precond_t / jnp.sqrt(mean + 1e-06)).T
     w_out[...] = p_scr[rows_of(block, 64), :].astype(BF16)
+
+    for t in (5, 6):
+        sum_copy(t).wait_recv()
+    tmp_q[...] += in_q[5].astype(F32) + in_q[6].astype(F32)
+    for h in range(HEADS):
+        dq_out[:, h * HEAD : (h + 1) * HEAD] = tmp_q[:, h * HEAD : (h + 1) * HEAD].T.astype(BF16)
 
     wait_recv(zk)
     dk_out[...] = z_total(dk_acc, dk_in, zin_k)

time: 97.5 us -> 87.8 us (0.901)
  Pallas kernels: 92.9 us -> 83.2 us
    pallas_call x1, Pallas kernels: 92.9 us -> 83.2 us  [per_device(): pl.pallas_call(kernel, out_shape=shapes, in_specs=[hbm] * 6, out_specs=(v...]
where the time goes in v3:
time: 87.8 us; the launch traced here: 87.5 us
  Pallas kernels  83.2 us (95%)
  local copies, waits for them, and re-layouts  3.68 us (4%)
    pallas_call x1, Pallas kernels, per_device(): pl.pallas_call(kernel, out_shape=shapes, in_specs=[hbm] * 6, out_specs=(v...  83.2 us
    unnamed x10, local copies, waits for them, and re-layouts  3.68 us

profile of v3, /device:TPU:1, one launch (start us, length us, event | category | flops | bytes accessed | tf_op | source)
XLA Modules:
  0.0 87.5 jit_solution(123632677835098962)
XLA Ops:
  0.6 83.2 %shard_map.93 = (bf16[128,512]{1,0:T(8,128)(2,1)}, bf16[128,128]{1,0:T(8,128)(2,1)}, bf16[128,128]{1,0:T(8,128)(2,1)}, bf16[64,128]{1,0:T(8,128)(2,1)}) custom-call(bf16[128,512]{1,0:T(8,128)(2,1)} %q_ref.1, bf16[128,128]{1,0:T(8,128)(2,1)} %k_ref.1, bf16[128,128]{1,0:T(8,128)(2,1)} %v_ref.1, bf16[128,512]{1,0:T(8,128)(2,1)} %o_ref.1, ...), custom_call_target="tpu_custom_call" | custom-call | tf_op jit(solution)/shard_map/pallas_call | solution.py:507
  83.8 0.0 copy-start.1
  83.8 1.6 %copy.14 = bf16[128,512]{1,0:T(8,128)(2,1)} copy(bf16[128,512]{1,0:T(8,128)(2,1)} %get-tuple-element.8) | data formatting | bytes 262144
  85.4 0.0 copy-done.1
  85.4 0.0 copy-start
  85.4 0.6 copy.15
  86.0 0.2 copy-done
  86.2 0.0 copy-start.2
  86.2 0.6 copy.16
  86.8 0.1 copy-done.2
  86.9 0.6 copy.17
Async XLA Ops:
  83.8 1.6 %copy-start.1 = (bf16[128,128]{1,0:T(8,128)(2,1)S(1)}, bf16[128,128]{1,0:T(8,128)(2,1)}, u32[]{:S(2)}) copy-start(bf16[128,128]{1,0:T(8,128)(2,1)} %get-tuple-element.9) | copy-start | bytes 98308
  85.4 0.8 copy-start
  86.2 0.7 copy-start.2

commit v4 on v3

--- a/solution.py
+++ b/solution.py
@@ -20,7 +20,7 @@
 NT = (((1,), (1,)), ((), ()))
 
 GROUPS = dict(
-    KZ=3, VZ=3, KC=4, VC=4, RQ=7, RD=7, ST=7, XZ=3, DVC=1, ZV=3, VG=3, WC=1, WY=7, WZ=3, GC=1, RS=7, DKC=1, ZK=3
+    KZ=3, VZ=3, KC=4, VC=4, RQ=8, RD=8, ST=7, DT=7, XZ=2, XR=2, XP=2, DVC=1, ZV=3, VG=3, WC=1, WY=7, WZ=3, GC=1, RS=7, DKC=1, ZK=3
 )
 BASE, N_SEMS = {}, 0
 for _name, _count in GROUPS.items():
@@ -39,10 +39,10 @@
 def kernel(
     q_ref, k_ref, v_ref, o_ref, do_ref, x_ref,
     dq_out, dk_out, dv_out, w_out,
-    qs, dos, obuf, kl, vl, kt, xin, xs, xw, ptil,
-    tops, stat, stat_in, factor, delta, dv_acc, dk_acc, tmp_q, out_q, in_q,
+    qs, dos, obuf, kl, vl, kt, xin, xs, xw, passing, ptil,
+    tops, stat, stat_in, own_delta, delta_in, factor, delta, dv_acc, dk_acc, tq, out_q, in_q,
     dv_send, dv_in, dk_send, dk_in, zout_v, zin_v, zout_k, zin_k, vg,
-    w_full, w_in, wk, wy_out, wy_in, gbuf, gbuf_in, gt, p_scr,
+    w_full, w_in, wk, wy_out, wy_in, wz_out, wz_in, gbuf, gbuf_in, gt, p_scr,
     send, recv, load,
 ):
     c = lax.axis_index("ctx")
@@ -117,6 +117,15 @@
         chunk = ring_arrival(t)
         copy(buf.at[chunk], buf.at[chunk], group, t, sibling).wait_recv()
 
+    def last_copies(buf, group):
+        up, down = buf.at[at_y(-3), 0:2], buf.at[at_y(3), 2:4]
+        return [copy(up, up, group, 6, ring_target(6)), copy(down, down, group, 7, ring_target(7))]
+
+    def last_wait(buf, group):
+        for n in range(2):
+            half = buf.at[at_y(4), 2 * n : 2 * n + 2]
+            copy(half, half, group, 6 + n, sibling).wait_recv()
+
     def block_copies(buf, group):
         mine = buf.at[rows_of(block, 128)]
         return [copy(mine, mine, group, i - 1, dev(y, at_z(i), core)) for i in range(1, Z)]
@@ -137,11 +146,7 @@
     for t in range(2):
         ring_copy(qs, "RQ", t).start()
     start([core_copy(kl, "KC", 0)])
-    for one in loads[5:9]:
-        one.wait()
-    for t in range(2):
-        ring_copy(dos, "RD", t).start()
-    for one in loads[9:]:
+    for one in loads[5:]:
         one.wait()
     start(block_copies(vl, "VZ"))
     start([core_copy(vl, "VC", 0)])
@@ -152,7 +157,7 @@
     dk_acc[...] = jnp.zeros(dk_acc.shape, F32)
     for h in range(HEADS):
         product = dos[y, h].astype(F32) * obuf[h].astype(F32)
-        stat[8:9, h * HEAD : (h + 1) * HEAD] = jnp.sum(product.T, axis=0, keepdims=True)
+        own_delta[h : h + 1, :] = jnp.sum(product.T, axis=0, keepdims=True)
 
     def arrange(i, _):
         for zz in range(Z):
@@ -160,10 +165,11 @@
         return 0
 
     lax.fori_loop(0, Y, arrange, 0)
-
-    for i in range(1, Z):
-        arrived_block(kl, "KZ", i)
-        start([core_copy(kl, "KC", Z - i)])
+    for t in range(2):
+        ring_copy(qs, "RQ", t).wait_send()
+    for t in range(2):
+        ring_copy(dos, "RD", t).start()
+    dt = start([copy(own_delta, delta_in.at[i - 1], "DT", i - 1, dev(at_y(i), z, core)) for i in range(1, Y)])
 
     def row_of(ref, chunk, cols):
         number = lax.broadcasted_iota(jnp.int32, (Y, 256), 0)
@@ -190,45 +196,40 @@
             put_row(stat, chunk, cols, top + jnp.log2(jnp.sum(e, axis=0, keepdims=True)))
 
     def pass_on(buf, group, t):
-        ring_wait(buf, group, t)
-
-        @pl.when(t + 1 < 7)
-        def _():
-            ring_wait(buf, group, t + 1)
-
-        @pl.when(t + 2 < 7)
-        def _():
-            ring_copy(buf, group, t + 2).start()
-
-        @pl.when(t + 3 < 7)
-        def _():
-            ring_copy(buf, group, t + 3).start()
+        for n in range(2):
+            ring_wait(buf, group, t + n)
+
+        onward = [ring_copy(buf, group, t + 2 + n) for n in range(2)] if t < 4 else last_copies(buf, group)
+        for one in onward:
+            one.start()
 
     def gather_step(n, _):
-        t = jnp.maximum(n - 1, 0)
-
-        @pl.when(jnp.logical_or(n == 0, jnp.logical_and(n > 1, lax.rem(t, 2) == 0)))
-        def _():
-            pass_on(qs, "RQ", t)
+        for when, buf, group, t in (
+            (0, qs, "RQ", 0), (1, dos, "RD", 0), (3, qs, "RQ", 2), (4, dos, "RD", 2), (5, qs, "RQ", 4), (7, dos, "RD", 4)
+        ):
+            @pl.when(n == when)
+            def _(buf=buf, group=group, t=t):
+                pass_on(buf, group, t)
 
         @pl.when(n == 0)
         def _():
+            for i in range(1, Z):
+                arrived_block(kl, "KZ", i)
+                start([kc[Z - i]])
             for i in range(Z):
                 core_wait(kl, "KC", i)
+            start(relay)
             forward(y, True)
 
-        @pl.when(jnp.logical_or(n == 0, jnp.logical_and(n > 2, lax.rem(n, 2) == 0)))
-        def _():
-            pass_on(dos, "RD", jnp.maximum(n - 2, 0))
-
         @pl.when(n == 2)
         def _():
-            for i in range(1, Z):
-                arrived_block(vl, "VZ", i)
-                start([vc[Z - i]])
             start(xz)
 
-        chunk = ring_arrival(t)
+        @pl.when(n == 7)
+        def _():
+            last_wait(qs, "RQ")
+
+        chunk = ring_arrival(jnp.maximum(n - 1, 0))
 
         @pl.when(jnp.logical_and(n > 0, chunk > y))
         def _():
@@ -236,26 +237,44 @@
 
         return 0
 
-    xz = [copy(xs.at[at_z(i)], xw.at[z], "XZ", i - 1, dev(y, at_z(i), core)) for i in range(1, Z)]
+    beside = (at_z(1), at_z(3))
+    xz = [copy(xs.at[beside[n]], xw.at[z], "XZ", n, dev(y, beside[n], core)) for n in range(2)]
+    wide = [pl.ds(0, 512), pl.ds(512, 512)]
+    relay = [
+        copy(xs.at[at_z(2), :, wide[n]], passing.at[n], "XR", n, dev(y, beside[n], core)) for n in range(2)
+    ]
+    relay_on = [
+        copy(passing.at[n], xw.at[beside[1 - n], :, wide[n]], "XP", n, dev(y, beside[n], core)) for n in range(2)
+    ]
+    kc = [core_copy(kl, "KC", i) for i in range(Z)]
     xw[z] = xs[z]
     vc = [core_copy(vl, "VC", i) for i in range(Z)]
     lax.fori_loop(0, 8, gather_step, 0)
 
     st = start([copy(stat, stat_in.at[i - 1], "ST", i - 1, dev(at_y(i), z, core)) for i in range(1, Y)])
-    ring_wait(dos, "RD", 6)
+    for i in range(1, Z):
+        arrived_block(vl, "VZ", i)
+        start([vc[Z - i]])
+    wait_recv(relay)
+    start(relay_on)
+    last_wait(dos, "RD")
     kt[...] = kl[...].astype(F32).T.astype(BF16)
     wait_recv(st)
-    parts = [stat[0:8, :]] + [stat_in[i, 0:8, :] for i in range(Y - 1)]
+    wait_recv(dt)
+    parts = [stat[...]] + [stat_in[i] for i in range(Y - 1)]
     high = parts[0]
     for part in parts[1:]:
         high = jnp.maximum(high, part)
     total = sum(jnp.exp2(part - high) for part in parts)
     factor[...] = jnp.exp2(tops[...] - (high + jnp.log2(total)))
     number = lax.broadcasted_iota(jnp.int32, (Y, 512), 0)
-    all_delta = jnp.where(number == y, stat[8:9, :], 0.0)
-    for i in range(1, Y):
-        all_delta = jnp.where(number == at_y(Y - i), stat_in[i - 1, 8:9, :], all_delta)
-    delta[...] = all_delta
+    delta[...] = jnp.zeros(delta.shape, F32)
+    for h in range(HEADS):
+        cols = slice(h * HEAD, (h + 1) * HEAD)
+        part = jnp.where(number[:, cols] == y, own_delta[h : h + 1, :], 0.0)
+        for i in range(1, Y):
+            part = jnp.where(number[:, cols] == at_y(Y - i), delta_in[i - 1, h : h + 1, :], part)
+        delta[:, cols] = part
 
     def value_tile(chunk):
         for n, cols in enumerate(halves):
@@ -299,7 +318,7 @@
     wc = [copy(w_full.at[rows_of(1 - core, 64)], w_in, "WC", 0, sibling)]
     wy = [copy(wy_out.at[i - 1], wy_in.at[i - 1], "WY", i - 1, dev(at_y(i), z, core)) for i in range(1, Y)]
 
-    wz = [copy(gbuf.at[z], gbuf.at[z], "WZ", i - 1, dev(y, at_z(i), core)) for i in range(1, Z)]
+    wz = [copy(wz_out, wz_in.at[i - 1], "WZ", i - 1, dev(y, at_z(i), core)) for i in range(1, Z)]
     gc = [copy(gbuf, gbuf_in, "GC", 0, sibling)]
 
     def chain_1():
@@ -315,7 +334,7 @@
 
     def chain_3():
         wait_recv(vgc)
-        wait_recv(xz)
+        wait_recv(xz + relay_on)
         value_t = vg[...].reshape(512, HEAD).astype(F32).T.astype(BF16)
         for n in range(4):
             cols = slice(n * 256, (n + 1) * 256)
@@ -337,13 +356,16 @@
         for i in range(Y - 1):
             g = g + wy_in[i].astype(F32)
         gbuf[z] = g
+        wz_out[...] = g.astype(BF16)
         start(wz)
 
     def chain_6():
         wait_recv(wz)
+        for i in range(1, Z):
+            gbuf[at_z(Z - i)] = wz_in[i - 1].astype(F32)
         start(gc)
 
-    def tile(chunk):
+    def tile(t, chunk):
         for n, cols in enumerate(halves):
             q2 = qs[chunk, 2 * n : 2 * n + 2].reshape(256, HEAD)
             do2 = dos[chunk, 2 * n : 2 * n + 2].reshape(256, HEAD)
@@ -351,7 +373,7 @@
             dp = dot(vl[...], do2, NT)
             ds = (p * (dp - row_of(delta, chunk, cols)) * SCALE).astype(BF16)
             dk_acc[...] += dot(ds, q2)
-            tmp_q[:, cols] = dot(kt[...], ds)
+            tq[t, :, cols] = dot(kt[...], ds)
 
     def sum_copy(t):
         return copy(out_q.at[t], in_q.at[t], "RS", t, ring_target(t))
@@ -359,41 +381,63 @@
     for i in range(Z):
         core_wait(vl, "VC", i)
 
-    def tile_step(t, _):
+    def ring_sum(t):
+        total = tq[t]
+        if t >= 2:
+            sum_copy(t - 2).wait_recv()
+            total = total + in_q[t - 2].astype(F32)
+        out_q[t] = total.astype(BF16)
+        sum_copy(t).start()
+
+    def tile_step(n, _):
+        t = jnp.where(n < 2, n, jnp.where(n == 2, 7, n - 1))
         s = t // 2
         chunk = jnp.where(t == 7, y, jnp.where(lax.rem(t, 2) == 0, at_y(4 - s), at_y(s - 3)))
 
+        @pl.when(n == 5)
+        def _():
+            chain_2()
+
         @pl.when(chunk >= y)
         def _():
-            tile(chunk)
+            tile(t, chunk)
 
         @pl.when(chunk < y)
         def _():
-            tmp_q[...] = jnp.zeros(tmp_q.shape, F32)
-
-        for when, chain in ((2, chain_2), (4, chain_4), (6, chain_5)):
-            pl.when(t == when)(chain)
-
-        @pl.when(jnp.logical_and(t >= 2, t < 7))
-        def _():
-            sum_copy(t - 2).wait_recv()
-            tmp_q[...] += in_q[t - 2].astype(F32)
-
-        @pl.when(t < 7)
-        def _():
-            out_q[t] = tmp_q[...].astype(BF16)
-            sum_copy(t).start()
-
-        for when, chain in ((0, chain_1), (3, chain_3), (7, chain_6)):
-            pl.when(t == when)(chain)
+            tq[t] = jnp.zeros((HEAD, 512), F32)
+
+        for when, done in ((0, 0), (1, 1), (3, 2), (4, 3)):
+            @pl.when(n == when)
+            def _(done=done):
+                ring_sum(done)
+
+        @pl.when(n == 0)
+        def _():
+            chain_1()
+
         return 0
 
     lax.fori_loop(0, 8, tile_step, 0)
 
     split_cores(dk_acc, dk_send)
     dkc = start([copy(dk_send, dk_in, "DKC", 0, sibling)])
+    ring_sum(4)
+    ring_sum(5)
+    chain_3()
     wait_recv(dkc)
     zk = start(z_sums(dk_acc, dk_in, zout_k, zin_k, "ZK"))
+    chain_4()
+    ring_sum(6)
+    chain_5()
+    for t in (5, 6):
+        sum_copy(t).wait_recv()
+    for h in range(HEADS):
+        cols = slice(h * HEAD, (h + 1) * HEAD)
+        total = tq[7, :, cols] + in_q[5, :, cols].astype(F32) + in_q[6, :, cols].astype(F32)
+        dq_out[:, cols] = total.T.astype(BF16)
+    wait_recv(zk)
+    dk_out[...] = z_total(dk_acc, dk_in, zin_k)
+    chain_6()
 
     wait_recv(gc)
     for zz in range(Z):
@@ -431,24 +475,17 @@
     p_scr[...] = (precond_t / jnp.sqrt(mean + 1e-06)).T
     w_out[...] = p_scr[rows_of(block, 64), :].astype(BF16)
 
-    for t in (5, 6):
-        sum_copy(t).wait_recv()
-    tmp_q[...] += in_q[5].astype(F32) + in_q[6].astype(F32)
-    for h in range(HEADS):
-        dq_out[:, h * HEAD : (h + 1) * HEAD] = tmp_q[:, h * HEAD : (h + 1) * HEAD].T.astype(BF16)
-
-    wait_recv(zk)
-    dk_out[...] = z_total(dk_acc, dk_in, zin_k)
-
     for one in sent:
         one.wait_send()
 
-    def finish(t, _):
-        for one in (ring_copy(qs, "RQ", t), ring_copy(dos, "RD", t), sum_copy(t)):
-            one.wait_send()
-        return 0
-
-    lax.fori_loop(0, 7, finish, 0)
+    for one in last_copies(qs, "RQ") + last_copies(dos, "RD") + [sum_copy(6)]:
+        one.wait_send()
+
+    for t in range(2, 6):
+        ring_copy(qs, "RQ", t).wait_send()
+    for t in range(6):
+        ring_copy(dos, "RD", t).wait_send()
+        sum_copy(t).wait_send()
 
 
 def per_device(queries, keys, values, saved_out, grad_out, layer_in):
@@ -465,15 +502,18 @@
         pltpu.VMEM((128, 4096), BF16),
         pltpu.VMEM((Z, 128, 1024), BF16),
         pltpu.VMEM((Z, 128, 1024), BF16),
+        pltpu.VMEM((2, 128, 512), BF16),
         pltpu.VMEM((Y, 2, KEYS, 256), F32),
         pltpu.VMEM((Y, 512), F32),
-        pltpu.VMEM((16, 512), F32),
-        pltpu.VMEM((Y - 1, 16, 512), F32),
+        pltpu.VMEM((Y, 512), F32),
+        pltpu.VMEM((Y - 1, Y, 512), F32),
+        pltpu.VMEM((8, HEAD), F32),
+        pltpu.VMEM((Y - 1, 8, HEAD), F32),
         pltpu.VMEM((Y, 512), F32),
         pltpu.VMEM((Y, 512), F32),
         pltpu.VMEM((KEYS, HEAD), F32),
         pltpu.VMEM((KEYS, HEAD), F32),
-        pltpu.VMEM((HEAD, 512), F32),
+        pltpu.VMEM((8, HEAD, 512), F32),
         pltpu.VMEM((7, HEAD, 512), BF16),
         pltpu.VMEM((7, HEAD, 512), BF16),
         pltpu.VMEM((Z, 128, HEAD), F32),
@@ -490,6 +530,8 @@
         pltpu.VMEM((Y, 64, 128), F32),
         pltpu.VMEM((7, 64, 128), BF16),
         pltpu.VMEM((7, 64, 128), BF16),
+        pltpu.VMEM((64, 128), BF16),
+        pltpu.VMEM((3, 64, 128), BF16),
         pltpu.VMEM((Z, 64, 128), F32),
         pltpu.VMEM((Z, 64, 128), F32),
         pltpu.VMEM((HEAD, BLOCK_ROWS), F32),

time: 87.8 us -> 81.5 us (0.928)
  Pallas kernels: 83.2 us -> 76.9 us
    pallas_call x1, Pallas kernels: 83.2 us -> 76.9 us  [per_device(): pl.pallas_call(kernel, out_shape=shapes, in_specs=[hbm] * 6, out_specs=(v...]
where the time goes in v4:
time: 81.5 us; the launch traced here: 81.2 us
  Pallas kernels  76.9 us (94%)
  local copies, waits for them, and re-layouts  3.68 us (5%)
    pallas_call x1, Pallas kernels, per_device(): pl.pallas_call(kernel, out_shape=shapes, in_specs=[hbm] * 6, out_specs=(v...  76.9 us
    unnamed x10, local copies, waits for them, and re-layouts  3.68 us

profile of v4, /device:TPU:1, one launch (start us, length us, event | category | flops | bytes accessed | tf_op | source)
XLA Modules:
  0.0 81.2 jit_solution(8924407156693876016)
XLA Ops:
  0.6 76.9 %shard_map.93 = (bf16[128,512]{1,0:T(8,128)(2,1)}, bf16[128,128]{1,0:T(8,128)(2,1)}, bf16[128,128]{1,0:T(8,128)(2,1)}, bf16[64,128]{1,0:T(8,128)(2,1)}) custom-call(bf16[128,512]{1,0:T(8,128)(2,1)} %q_ref.1, bf16[128,128]{1,0:T(8,128)(2,1)} %k_ref.1, bf16[128,128]{1,0:T(8,128)(2,1)} %v_ref.1, bf16[128,512]{1,0:T(8,128)(2,1)} %o_ref.1, ...), custom_call_target="tpu_custom_call" | custom-call | tf_op jit(solution)/shard_map/pallas_call | solution.py:549
  77.5 0.0 copy-start.1
  77.5 1.6 %copy.14 = bf16[128,512]{1,0:T(8,128)(2,1)} copy(bf16[128,512]{1,0:T(8,128)(2,1)} %get-tuple-element.8) | data formatting | bytes 262144
  79.1 0.0 copy-done.1
  79.1 0.0 copy-start
  79.1 0.6 copy.15
  79.7 0.2 copy-done
  79.9 0.0 copy-start.2
  79.9 0.6 copy.16
  80.5 0.1 copy-done.2
  80.6 0.6 copy.17
Async XLA Ops:
  77.5 1.6 %copy-start.1 = (bf16[128,128]{1,0:T(8,128)(2,1)S(1)}, bf16[128,128]{1,0:T(8,128)(2,1)}, u32[]{:S(2)}) copy-start(bf16[128,128]{1,0:T(8,128)(2,1)} %get-tuple-element.9) | copy-start | bytes 98308
  79.1 0.8 copy-start
  79.9 0.7 copy-start.2

commit v5 on v4

--- a/solution.py
+++ b/solution.py
@@ -165,8 +165,6 @@
         return 0
 
     lax.fori_loop(0, Y, arrange, 0)
-    for t in range(2):
-        ring_copy(qs, "RQ", t).wait_send()
     for t in range(2):
         ring_copy(dos, "RD", t).start()
     dt = start([copy(own_delta, delta_in.at[i - 1], "DT", i - 1, dev(at_y(i), z, core)) for i in range(1, Y)])
@@ -481,7 +479,7 @@
     for one in last_copies(qs, "RQ") + last_copies(dos, "RD") + [sum_copy(6)]:
         one.wait_send()
 
-    for t in range(2, 6):
+    for t in range(6):
         ring_copy(qs, "RQ", t).wait_send()
     for t in range(6):
         ring_copy(dos, "RD", t).wait_send()

time: 81.5 us -> 81.5 us (level)
  no operation moved by 1% of the time
where the time goes in v5:
time: 81.5 us; the launch traced here: 81.2 us
  Pallas kernels  76.9 us (94%)
  local copies, waits for them, and re-layouts  3.68 us (5%)
    pallas_call x1, Pallas kernels, per_device(): pl.pallas_call(kernel, out_shape=shapes, in_specs=[hbm] * 6, out_specs=(v...  76.9 us
    unnamed x10, local copies, waits for them, and re-layouts  3.68 us

profile of v5, /device:TPU:1, one launch (start us, length us, event | category | flops | bytes accessed | tf_op | source)
XLA Modules:
  0.0 81.2 jit_solution(10464233357203729375)
XLA Ops:
  0.6 76.9 %shard_map.93 = (bf16[128,512]{1,0:T(8,128)(2,1)}, bf16[128,128]{1,0:T(8,128)(2,1)}, bf16[128,128]{1,0:T(8,128)(2,1)}, bf16[64,128]{1,0:T(8,128)(2,1)}) custom-call(bf16[128,512]{1,0:T(8,128)(2,1)} %q_ref.1, bf16[128,128]{1,0:T(8,128)(2,1)} %k_ref.1, bf16[128,128]{1,0:T(8,128)(2,1)} %v_ref.1, bf16[128,512]{1,0:T(8,128)(2,1)} %o_ref.1, ...), custom_call_target="tpu_custom_call" | custom-call | tf_op jit(solution)/shard_map/pallas_call | solution.py:547
  77.6 0.0 copy-start.1
  77.6 1.6 %copy.14 = bf16[128,512]{1,0:T(8,128)(2,1)} copy(bf16[128,512]{1,0:T(8,128)(2,1)} %get-tuple-element.8) | data formatting | bytes 262144
  79.1 0.0 copy-done.1
  79.1 0.0 copy-start
  79.1 0.6 copy.15
  79.8 0.2 copy-done
  79.9 0.0 copy-start.2
  79.9 0.6 copy.16
  80.5 0.1 copy-done.2
  80.6 0.6 copy.17
Async XLA Ops:
  77.6 1.6 %copy-start.1 = (bf16[128,128]{1,0:T(8,128)(2,1)S(1)}, bf16[128,128]{1,0:T(8,128)(2,1)}, u32[]{:S(2)}) copy-start(bf16[128,128]{1,0:T(8,128)(2,1)} %get-tuple-element.9) | copy-start | bytes 98308
  79.1 0.8 copy-start
  79.9 0.7 copy-start.2
